TPU v7x, 128 devices: a whole 4x4x4 slice. The times are simulated.
128 devices in a mesh: enc: 2 (over y_lo), fsdp: 64 (over x, y_hi, z, core).
Axes of the slice: x: 4, y: 4 (y_hi: 2, y_lo: 2; y = y_hi * 2 + y_lo), z: 4, core: 2. Of those that a mesh axis runs over, the one named last changes fastest.
Arguments:
- dino_feats: bfloat16 [128, 2, 256, 1024], P('fsdp', 'enc'), may hold values from -16 to 16
- siglip_feats: bfloat16 [128, 2, 256, 1152], P('fsdp', 'enc'), may hold values from -16 to 16
- proj_weight: bfloat16 [2176, 4352], P('fsdp', 'enc'), may hold values from -0.125 to 0.125
- proj_bias: float32 [4352], P('enc'), may hold values from -3 to 3
- hidden_grad: bfloat16 [128, 512, 4352], P('fsdp', None, 'enc'), may hold values from -6 to 6
Outputs:
- hidden: bfloat16 [128, 512, 4352], P('fsdp', None, 'enc')
- weight_grad: float32 [2176, 4352], P('fsdp', 'enc')
- bias_grad: float32 [4352], P('enc')
- dino_grad: bfloat16 [128, 2, 256, 1024], P('fsdp', 'enc')
- siglip_grad: bfloat16 [128, 2, 256, 1152], P('fsdp', 'enc')
All inputs are finite; a program needn't handle non-finite values.
Results may differ from a plain program's by a relative error of at most 0.0059.
Values may be sent and summed in bfloat16 or wider, within the bound.
A program may use at most 192 MiB of HBM per device.

v0:
```python
import jax
import jax.numpy as jnp
from jax import lax
from jax.sharding import Mesh
from jax.sharding import PartitionSpec as P

DINO = 1024
FEAT = 2176
FSDP = ("fsdp_0", "fsdp_1", "fsdp_2", "fsdp_3")


def sent_together(arrays, axis, dim, along):
    ends, at = ([], 0)
    for a in arrays[:-1]:
        at += a.shape[along]
        ends.append(at)
    both = jnp.concatenate(arrays, axis=along)
    return tuple(jnp.split(lax.all_gather(both, axis, axis=dim, tiled=True), ends, axis=along))


def split_up(array, dim, length):
    before, after = (array.shape[:dim], array.shape[dim + 1 :])
    return jnp.moveaxis(array.reshape(*before, length, -1, *after), dim, 0)


def sum_by_chip_2(array, chips, core, dim):
    sizes = (lax.axis_size(chips), lax.axis_size(core))
    pieces = split_up(array, dim, sizes[0] * sizes[1])
    inside = pieces.shape[1:]
    pieces = pieces.reshape(*sizes, *inside).swapaxes(0, 1).reshape(-1, *inside)
    pieces = lax.psum_scatter(pieces, core, scatter_dimension=0, tiled=True)
    return lax.psum_scatter(pieces, chips, scatter_dimension=0, tiled=True)[0]


def sent_to_all(array, axis):
    length = lax.axis_size(axis)
    return lax.all_to_all(
        jnp.broadcast_to(array[None], (length, *array.shape)), axis, 0, 0, tiled=True
    )


def taken_together(array, axis):
    return sent_to_all(array, axis).sum(axis=0)


def swapped(array, axis, bit):
    return lax.ppermute(array, axis, [(i, i ^ 1 << bit) for i in range(lax.axis_size(axis))])


def gelu_exact(values):
    return jax.nn.gelu(values, approximate=False)


def shards(dino_feats, siglip_feats, proj_weight, proj_bias, hidden_grad):
    dino_pair, siglip_pair = sent_together((dino_feats, siglip_feats), "enc", 1, 3)
    lead_shape = dino_pair.shape[:3]
    feats = jnp.concatenate([dino_pair, siglip_pair], -1).reshape(-1, FEAT)
    width = proj_weight.shape[1]
    whole_weight = lax.all_gather(proj_weight, FSDP, axis=0, tiled=True)
    preact = jnp.dot(feats, whole_weight, preferred_element_type=jnp.float32)
    preact = preact + proj_bias
    activated, pull = jax.vjp(gelu_exact, preact)
    hidden_out = activated.astype(jnp.bfloat16).reshape(hidden_grad.shape)
    (local_grad,) = pull(hidden_grad.reshape(-1, width).astype(jnp.float32))
    local_grad = local_grad.astype(jnp.bfloat16)
    weight_grad = sum_by_chip_2(
        lax.dot_general(
            feats, local_grad, (((0,), (0,)), ((), ())), preferred_element_type=jnp.float32
        ),
        ("fsdp_0", "fsdp_1", "fsdp_2"),
        "fsdp_3",
        0,
    )
    bias_grad = taken_together(jnp.sum(local_grad.astype(jnp.float32), 0), FSDP)
    feat_part = lax.dot_general(
        local_grad, whole_weight, (((1,), (1,)), ((), ())), preferred_element_type=jnp.float32
    )
    feat_part = feat_part.astype(jnp.bfloat16).reshape(lead_shape + (FEAT,))
    own_image = lax.axis_index("enc")
    kept_half = lax.dynamic_slice_in_dim(feat_part, own_image, 1, 1)
    sent_half = lax.dynamic_slice_in_dim(feat_part, 1 - own_image, 1, 1)
    other_half = swapped(sent_half, "enc", 0)
    feat_grad = (kept_half.astype(jnp.float32) + other_half.astype(jnp.float32)).astype(
        jnp.bfloat16
    )
    return (hidden_out, weight_grad, bias_grad, feat_grad[..., :DINO], feat_grad[..., DINO:])


def solution(mesh):
    finer = Mesh(
        mesh.devices.reshape(mesh.shape["enc"], 4, 2, 4, 2),
        ("enc", "fsdp_0", "fsdp_1", "fsdp_2", "fsdp_3"),
    )
    in_specs = (
        P(FSDP, "enc", None, None),
        P(FSDP, "enc", None, None),
        P(FSDP, "enc"),
        P("enc"),
        P(FSDP, None, "enc"),
    )
    out_specs = (
        P(FSDP, None, "enc"),
        P(FSDP, "enc"),
        P("enc"),
        P(FSDP, "enc", None, None),
        P(FSDP, "enc", None, None),
    )
    return jax.shard_map(
        shards, mesh=finer, in_specs=in_specs, out_specs=out_specs, check_vma=False
    )
```

profile of v0, /device:TPU:0, one launch (start us, length us, event | category | flops | bytes accessed | tf_op | source)
XLA Modules:
  0.0 689.9 jit_solution(7756643836204835596)
XLA Ops:
  7.2 0.0 all-gather.4.cloned.1.call-start
  7.2 3.1 pad_maximum_fusion
  10.3 0.0 all-gather.4.cloned.1.call-update
  10.3 0.0 all-gather.6.cloned.1.call-start
  10.4 0.7 all-gather.6.cloned.1.call-update
  11.1 0.0 reduce-scatter.3.cloned.1.call-start
  11.1 64.1 %all-gather.4.cloned.1.call-done = bf16[2,2,256,2176]{3,2,1,0:T(8,128)(2,1)} async-done(((bf16[2,1,256,2176]{3,2,1,0:T(8,128)(2,1)}), bf16[2,2,256,2176]{3,2,1,0:T(8,128)(2,1)}) %all-gather.4.cloned.1.call-update) | async-done | bytes 4456464 | tf_op jit(solution)/shard_map/all_gather | solution.py:18
  75.2 6.5 copy.17
  81.7 7.3 %dot_general.15 = bf16[32,2,34,1024]{3,2,1,0:T(8,128)(2,1)} reshape(bf16[2176,1024]{1,0:T(8,128)(2,1)} %bitcast.27) | data formatting | bytes 8912896 | tf_op jit(solution)/shard_map/dot_general | solution.py:67
  89.0 0.0 copy-start.1
  89.0 80.0 %all-gather.6.cloned.1.call-done = bf16[64,34,2176]{2,1,0:T(8,128)(2,1)} async-done(((bf16[1,34,2176]{2,1,0:T(8,128)(2,1)}), bf16[64,34,2176]{2,1,0:T(8,128)(2,1)}) %all-gather.6.cloned.1.call-update) | async-done | bytes 9469968 | tf_op jit(solution)/shard_map/all_gather | solution.py:59
  169.0 13.7 %reshape.39 = bf16[2176,2176]{1,0:T(8,128)(2,1)} reshape(bf16[64,34,2176]{2,1,0:T(8,128)(2,1)} %all-gather.6.cloned.1.call-done) | data formatting | bytes 18939904
  182.7 0.0 copy-done.1
  182.7 42.3 %convert_reduce_fusion = (f32[2176]{0:T(1024)S(1)}, bf16[1024,2176]{1,0:T(8,128)(2,1)}, f32[1024,2176]{1,0:T(8,128)}, f32[1024,2176]{1,0:T(8,128)}) fusion(bf16[2,512,2176]{2,1,0:T(8,128)(2,1)} %param.9, f32[2176]{0:T(1024)S(1)} %copy-done.1, bf16[1024,2176]{1,0:T(8,128)(2,1)} %bitcast.30, bf16[2176,2176]{1,0:T(8,128)(2,1)} %reshape.39), kind=kOutput, calls=%fused_computation.12 | convolution fusion | flops 9866573824 | bytes 40682496 | tf_op jit(solution)/shard_map/dot_general | solution.py:60
  225.0 15.9 %convolution_bitcast_fusion = f32[2,32,34,2176]{3,2,0,1:T(8,128)S(1)} fusion(bf16[32,2,34,1024]{3,2,1,0:T(8,128)(2,1)} %dot_general.15, bf16[1024,2176]{1,0:T(8,128)(2,1)} %get-tuple-element.6), kind=kOutput, calls=%fused_computation.1 | convolution fusion | flops 9697230848 | bytes 27852800 | tf_op jit(solution)/shard_map/dot_general | solution.py:67
  240.9 12.0 %copy.18 = f32[2,32,34,2176]{3,1,0,2:T(8,128)} copy(f32[2,32,34,2176]{3,2,0,1:T(8,128)S(1)} %convolution_bitcast_fusion) | data formatting | bytes 37879808 | tf_op jit(solution)/shard_map/transpose | solution.py:30
  252.9 0.0 reduce-scatter.3.cloned.1.call-update
  252.9 0.0 all-reduce.3.cloned.1.call-start
  253.0 28.9 %reduce-scatter.3.cloned.1.call-done = f32[32,34,2176]{2,0,1:T(8,128)} async-done(((f32[64,34,2176]{2,0,1:T(8,128)}), f32[32,34,2176]{2,0,1:T(8,128)}) %reduce-scatter.3.cloned.1.call-update) | async-done | bytes 9469968 | tf_op jit(solution)/shard_map/reduce_scatter | solution.py:31
  281.9 0.0 all-reduce.3.cloned.1.call-update
  281.9 0.0 copy-start.2
  281.9 14.9 %convolution_convert_fusion = bf16[1024,2176]{1,0:T(8,128)(2,1)S(1)} fusion(bf16[1024,2176]{1,0:T(8,128)(2,1)} %get-tuple-element.6, bf16[2176,2176]{1,0:T(8,128)(2,1)} %reshape.39), kind=kOutput, calls=%fused_computation.27 | convolution fusion | flops 9699459072 | bytes 18382848 | tf_op jit(solution)/shard_map/dot_general | solution.py:75
  296.8 0.0 copy-start
  296.8 2.2 copy-done
  299.0 0.2 constant_dynamic-slice_fusion.1
  299.2 1.7 collective-permute-start
  300.9 0.0 copy-done.2
  300.9 0.6 dynamic-slice
  301.5 1.1 broadcast_in_dim.2
  302.6 10.0 %all-to-all-start = ((f32[64,1,2176]{2,1,0:T(1,128)}), f32[64,1,2176]{2,1,0:T(1,128)S(1)}, u32[]{:S(2)}, u32[]{:S(2)}) async-start(f32[64,1,2176]{2,1,0:T(1,128)} %broadcast_in_dim.2), calls=%async_computation.1 | async-start | bytes 1114112 | tf_op jit(solution)/shard_map/all_to_all | solution.py:37
  312.6 9.3 %multiply_convert_fusion = bf16[1024,2176]{1,0:T(8,128)(2,1)} fusion(f32[1024,2176]{1,0:T(8,128)} %get-tuple-element.7, f32[1024,2176]{1,0:T(8,128)} %get-tuple-element.8, f32[2176]{0:T(1024)S(1)} %copy-done.1), kind=kLoop, calls=%fused_computation.13 | loop fusion | flops 8912896 | bytes 22290944 | tf_op jit(solution)/shard_map/convert_element_type | solution.py:63
  321.8 95.2 %all-to-all-done = f32[64,1,2176]{2,1,0:T(1,128)S(1)} async-done(((f32[64,1,2176]{2,1,0:T(1,128)}), f32[64,1,2176]{2,1,0:T(1,128)S(1)}, u32[]{:S(2)}, u32[]{:S(2)}) %all-to-all-start) | async-done | bytes 557088 | tf_op jit(solution)/shard_map/all_to_all | solution.py:37
  417.0 1.0 reduce_sum.19
  418.0 0.0 collective-permute-done
  418.0 2.9 add_convert_fusion
  420.9 1.1 slice.10
  422.0 1.1 slice.9
  423.1 257.0 %all-reduce.3.cloned.1.call-done = f32[32,34,2176]{2,0,1:T(8,128)} async-done(((f32[32,34,2176]{2,0,1:T(8,128)}), f32[32,34,2176]{2,0,1:T(8,128)}) %all-reduce.3.cloned.1.call-update) | async-done | bytes 9469968
  680.1 2.5 constant_dynamic-slice_fusion
  682.6 0.8 copy.26
Async XLA Ops:
  7.2 68.0 %all-gather.4.cloned.1.call-start = ((), (), s32[]{:S(2)}) async-start(), calls=%async_computation.2 | async-start | bytes 6684672 | tf_op jit(solution)/shard_map/all_gather | solution.py:18
  10.3 158.6 %all-gather.6.cloned.1.call-start = ((), (), s32[]{:S(2)}) async-start(), calls=%async_computation.4 | async-start | bytes 11315200 | tf_op jit(solution)/shard_map/all_gather | solution.py:59
  11.1 270.8 %reduce-scatter.3.cloned.1.call-start = ((), (), s32[]{:S(2)}) async-start(), calls=%async_computation.3 | async-start | bytes 28409856 | tf_op jit(solution)/shard_map/reduce_scatter | solution.py:31
  89.0 93.8 %copy-start.1 = (f32[2176]{0:T(1024)S(1)}, f32[2176]{0:T(1024)}, u32[]{:S(2)}) copy-start(f32[2176]{0:T(1024)} %param.8) | copy-start | bytes 26116
  252.9 427.2 %all-reduce.3.cloned.1.call-start = ((), (), s32[]{:S(2)}) async-start(), calls=%async_computation.5 | async-start | bytes 18939904
  281.9 19.0 %copy-start.2 = (u32[128]{0:T(128)S(1)}, u32[128]{0:T(128)}, u32[]{:S(2)}) copy-start(u32[128]{0:T(128)} %constant.83) | copy-start | bytes 1540
  296.8 2.2 copy-start
  299.2 118.9 %collective-permute-start = (bf16[2,1,256,2176]{3,2,1,0:T(8,128)(2,1)S(1)}, bf16[2,1,256,2176]{3,2,1,0:T(8,128)(2,1)}, u32[]{:S(2)}, u32[]{:S(2)}) collective-permute-start(bf16[2,1,256,2176]{3,2,1,0:T(8,128)(2,1)S(1)} %constant_dynamic-slice_fusion.1), channel_id=1, source_target_pairs={{0,64},{64,0},{1,65},{65,1},{2,66},{66,2},{3,67},{67,3},{4,68},{68... | collective-permute-start | bytes 6684680 | tf_op jit(solution)/shard_map/ppermute | solution.py:47
  302.6 114.5 %all-to-all-start = ((f32[64,1,2176]{2,1,0:T(1,128)}), f32[64,1,2176]{2,1,0:T(1,128)S(1)}, u32[]{:S(2)}, u32[]{:S(2)}) async-start(f32[64,1,2176]{2,1,0:T(1,128)} %broadcast_in_dim.2), calls=%async_computation.1 | async-start | bytes 1114112 | tf_op jit(solution)/shard_map/all_to_all | solution.py:37
Sparse Core Ops, SparseCore 0:
  10.5 64.6 all-gather.3
  78.4 90.4 all-gather.5
  253.1 28.7 reduce-scatter.2
  284.3 395.7 all-reduce.2
where the time goes:
time: 691 us; the launch traced here: 690 us
  waiting for transfers between devices  526 us (76%)
  matrix products  73.1 us (11%)
  local copies, waits for them, and re-layouts  49 us (7%)
  other arithmetic  16.2 us (2%)
  between operations  13.8 us (2%)
  starting transfers between devices  11.8 us (2%)
    unnamed x5, waiting for transfers between devices  258 us
    all_to_all x1, waiting for transfers between devices, sent_to_all(): lax.all_to_all(jnp.broadcast_to(array[None], (length, *array.shape)), axi...  95.2 us
    all_gather x1, waiting for transfers between devices, shards(): whole_weight = lax.all_gather(proj_weight, FSDP, axis=0, tiled=True)  80 us
    all_gather x1, waiting for transfers between devices, sent_together(): lax.all_gather(both, axis, axis=dim, tiled=True)  64.1 us
    dot_general x1, matrix products, shards(): preact = jnp.dot(feats, whole_weight, preferred_element_type=jnp.float32)  42.3 us
    reduce_scatter x1, waiting for transfers between devices, sum_by_chip_2(): pieces = lax.psum_scatter(pieces, core, scatter_dimension=0, tiled=True)  28.9 us
    unnamed x10, local copies, waits for them, and re-layouts  19.8 us
    dot_general x1, matrix products, shards(): lax.dot_general(feats, local_grad, (((0,), (0,)), ((), ())), preferred_el...  15.9 us
  transfers between devices with their start and end apart: 6, of which 5 were waited for; matrix products, arithmetic and copies ran while one was open for 7% of the time, Pallas kernels for 0%

commit v1 on v0

v1 whole, which is shorter than its diff:
```python
import jax
import jax.numpy as jnp
from jax import lax
from jax.experimental import pallas as pl
from jax.experimental.pallas import tpu as pltpu
from jax.sharding import Mesh
from jax.sharding import PartitionSpec as P

E, X, Y, Z, C = "enc", "fsdp_0", "fsdp_1", "fsdp_2", "fsdp_3"
FSDP = (X, Y, Z, C)
DINO = 1024
SIG = 1152
FEAT = 2176
IMG = 256
ROWS = 34
WA = 1024
WB = 1152
GROUP = 8 * ROWS
F32 = jnp.float32
BF16 = jnp.bfloat16
COPIES = 80
LOCALS = 24


def kernel(
    dino, siglip, w, bias_in, hg,
    hidden, wgrad, bgrad, dino_grad, siglip_grad,
    ga, gb, wd, f, ft, lg, hid, fsend, frecv,
    rca, rcb, r1a, r2a, r1b, r2b, q1a, q2a, rya, q1b, q2b, ryb,
    scr, pre, wout, bias, bsum, bc, bz, bx, by,
    ssem, rsem, lsem,
):
    e, x, y, z, c = (lax.axis_index(n) for n in (E, X, Y, Z, C))
    xp, xm, xo = (lax.rem(x + k, 4) for k in (1, 3, 2))
    zp, zm, zo = (lax.rem(z + k, 4) for k in (1, 3, 2))
    yo, co, eo = 1 - y, 1 - c, 1 - e
    za, ua = z * 2 + c, x * 2 + y
    xb, ub = x * 2 + c, y * 4 + z

    counts = {"remote": 0, "local": 0}
    sends = []

    def remote(src, dst, axis, to):
        i = counts["remote"]
        counts["remote"] += 1
        copy = pltpu.make_async_remote_copy(
            src_ref=src, dst_ref=dst, send_sem=ssem.at[i], recv_sem=rsem.at[i],
            device_id={axis: to}, device_id_type=pl.DeviceIdType.MESH,
        )
        copy.start()
        sends.append(copy)
        return copy

    def local(src, dst):
        i = counts["local"]
        counts["local"] += 1
        copy = pltpu.make_async_copy(src, dst, lsem.at[i])
        copy.start()
        return copy

    def wait_sends():
        for copy in sends:
            copy.wait_send()
        sends.clear()

    own_w = [local(w.at[:, 0:WA], ga.at[za, ua]), local(w.at[:, WA:FEAT], gb.at[xb, ub])]
    own_f = []
    for b in range(2):
        own_f.append(local(dino.at[b, 0], f.at[b * IMG:(b + 1) * IMG, 0:DINO]))
        own_f.append(local(siglip.at[b, 0], f.at[b * IMG:(b + 1) * IMG, DINO:FEAT]))
    own_bias = local(bias_in, bias)

    barrier = pltpu.get_barrier_semaphore()
    peers = [(E, eo), (C, co), (Y, yo)]
    peers += [(X, k) for k in (xp, xm, xo)] + [(Z, k) for k in (zp, zm, zo)]
    for axis, to in peers:
        pl.semaphore_signal(
            barrier, inc=1, device_id={axis: to}, device_id_type=pl.DeviceIdType.MESH
        )
    pl.semaphore_wait(barrier, len(peers))

    for copy in own_w:
        copy.wait()
    a1 = remote(ga.at[za, ua], ga.at[za, ua], Y, yo)
    b1p = remote(gb.at[xb, ub], gb.at[xb, ub], Z, zp)
    b1m = remote(gb.at[xb, ub], gb.at[xb, ub], Z, zm)
    far_f = []
    for b in range(2):
        rows = slice(2 * IMG + b * IMG, 2 * IMG + (b + 1) * IMG)
        far_f.append(remote(dino.at[b, 0], f.at[rows, 0:DINO], E, eo))
        far_f.append(remote(siglip.at[b, 0], f.at[rows, DINO:FEAT], E, eo))
    own_hg = []
    for i, image in enumerate((e, eo)):
        for b in range(2):
            own_hg.append(
                local(
                    hg.at[b, pl.ds(pl.multiple_of(image * IMG, IMG), IMG)],
                    lg.at[(2 * i + b) * IMG:(2 * i + b + 1) * IMG],
                )
            )

    a1.wait_recv()
    pair = pl.ds(2 * x, 2)
    a2p = remote(ga.at[za, pair], ga.at[za, pair], X, xp)
    a2m = remote(ga.at[za, pair], ga.at[za, pair], X, xm)
    b1p.wait_recv()
    far = gb.at[xb, y * 4 + zm, :, 0:512]
    b2p = remote(far, far, Z, zp)
    b1m.wait_recv()
    far = gb.at[xb, y * 4 + zp, :, 512:WB]
    b2m = remote(far, far, Z, zm)
    a2p.wait_recv()
    far = ga.at[za, 2 * xm]
    a3p = remote(far, far, X, xp)
    a2m.wait_recv()
    far = ga.at[za, 2 * xp + 1]
    a3m = remote(far, far, X, xm)
    b2p.wait_recv()
    b2m.wait_recv()
    line = gb.at[xb, pl.ds(4 * y, 4)]
    b3 = remote(line, line, Y, yo)
    a3p.wait_recv()
    a3m.wait_recv()
    a4p = remote(ga.at[za], ga.at[za], Z, zp)
    a4m = remote(ga.at[za], ga.at[za], Z, zm)
    b3.wait_recv()
    b4p = remote(gb.at[xb], gb.at[xb], X, xp)
    b4m = remote(gb.at[xb], gb.at[xb], X, xm)
    shared = [remote(ga.at[za], ga.at[za], C, co), remote(gb.at[xb], gb.at[xb], C, co)]

    def transposed(first):
        def step(t, carry):
            cols = pl.ds(pl.multiple_of(t * 128, 128), 128)
            ft[cols, first:first + 512] = f[first:first + 512, cols].T
            return carry
        lax.fori_loop(0, FEAT // 128, step, 0)

    for copy in own_f:
        copy.wait()
    transposed(0)

    a4p.wait_recv()
    blk = zm * 2 + c
    a5p = remote(ga.at[blk, 0:4], ga.at[blk, 0:4], Z, zp)
    shared.append(remote(ga.at[blk], ga.at[blk], C, co))
    a4m.wait_recv()
    blk = zp * 2 + c
    a5m = remote(ga.at[blk, 4:8], ga.at[blk, 4:8], Z, zm)
    shared.append(remote(ga.at[blk], ga.at[blk], C, co))
    b4p.wait_recv()
    blk = xm * 2 + c
    b5p = remote(gb.at[blk, 0:4], gb.at[blk, 0:4], X, xp)
    shared.append(remote(gb.at[blk], gb.at[blk], C, co))
    b4m.wait_recv()
    blk = xp * 2 + c
    b5m = remote(gb.at[blk, 4:8], gb.at[blk, 4:8], X, xm)
    shared.append(remote(gb.at[blk], gb.at[blk], C, co))
    blka, blkb = zo * 2 + c, xo * 2 + c
    a5p.wait_recv()
    shared.append(remote(ga.at[blka, 0:4], ga.at[blka, 0:4], C, co))
    a5m.wait_recv()
    shared.append(remote(ga.at[blka, 4:8], ga.at[blka, 4:8], C, co))
    b5p.wait_recv()
    shared.append(remote(gb.at[blkb, 0:4], gb.at[blkb, 0:4], C, co))
    b5m.wait_recv()
    shared.append(remote(gb.at[blkb, 4:8], gb.at[blkb, 4:8], C, co))
    for copy in shared:
        copy.wait_recv()

    def where_b(g, j):
        return (g // 2) * 2 + j % 2, lax.rem(g, 2) * 4 + j // 2

    def assemble(g, carry):
        rows = pl.ds(pl.multiple_of(g * GROUP, 16), GROUP)
        for j in range(8):
            scr[j * ROWS:(j + 1) * ROWS, 0:WA] = ga[j, g].astype(F32)
        wd[rows, 0:WA] = scr[:, 0:WA].astype(BF16)
        for j in range(8):
            i, k = where_b(g, j)
            scr[j * ROWS:(j + 1) * ROWS, :] = gb[i, k].astype(F32)
        wd[rows, WA:FEAT] = scr[...].astype(BF16)
        return carry

    lax.fori_loop(0, 8, assemble, 0)
    wait_sends()

    bsum[...] = jnp.zeros_like(bsum)
    own_bias.wait()

    def forward(first):
        def tile(start, width):
            cols = pl.ds(start, width)
            pre[:, 0:width] = jnp.dot(
                f[first:first + 512, :], wd[:, cols], preferred_element_type=F32
            )

            def rows_step(r, acc):
                at = pl.ds(pl.multiple_of(r * 32, 32), 32)
                lat = pl.ds(pl.multiple_of(first + r * 32, 32), 32)
                v = pre[at, 0:width] + bias[:, cols]
                cdf = 0.5 + 0.5 * lax.erf(v * 0.7071067811865476)
                pdf = jnp.exp(v * v * -0.5) * 0.3989422804014327
                hid[at, cols] = (v * cdf).astype(BF16)
                grad = (lg[lat, cols].astype(F32) * (cdf + v * pdf)).astype(BF16)
                lg[lat, cols] = grad
                wide = grad.astype(F32)
                return acc + (wide[0:8] + wide[8:16] + wide[16:24] + wide[24:32])

            acc = lax.fori_loop(0, 16, rows_step, jnp.zeros((8, width), F32))
            bsum[:, cols] += jnp.sum(acc, axis=0, keepdims=True)

        def step(t, carry):
            tile(pl.multiple_of(t * 512, 512), 512)
            return carry

        lax.fori_loop(0, 4, step, 0)
        tile(2048, 128)

    def hidden_out(image):
        return [
            local(
                hid.at[b * IMG:(b + 1) * IMG],
                hidden.at[b, pl.ds(pl.multiple_of(image * IMG, IMG), IMG)],
            )
            for b in range(2)
        ]

    def feature_part(first, dst, start, width):
        dst[:, pl.ds(start, width)] = lax.dot_general(
            lg[first:first + 512, :], wd[pl.ds(start, width), :],
            (((1,), (1,)), ((), ())), preferred_element_type=F32,
        ).astype(BF16)

    def feature_half(first, dst, half):
        def step(t, carry):
            feature_part(first, dst, pl.multiple_of(half * 1024 + t * 512, 512), 512)
            return carry
        lax.fori_loop(0, 2, step, 0)
        if half == 1:
            feature_part(first, dst, 2048, 128)

    own_hg[0].wait()
    own_hg[1].wait()
    forward(0)
    outs = hidden_out(e)
    for copy in far_f:
        copy.wait_recv()
    transposed(512)
    own_hg[2].wait()
    own_hg[3].wait()
    for copy in outs:
        copy.wait()
    forward(512)
    outs = hidden_out(eo)
    feature_half(512, fsend, 0)
    back = [remote(fsend.at[:, 0:DINO], frecv.at[:, 0:DINO], E, eo)]
    feature_half(512, fsend, 1)
    back.append(remote(fsend.at[:, DINO:FEAT], frecv.at[:, DINO:FEAT], E, eo))

    bc[c] = bsum[...]
    bias_c = remote(bc.at[c], bc.at[c], C, co)

    def weight_part(g, carry, first, width):
        rows = pl.ds(pl.multiple_of(g * GROUP, 16), GROUP)
        scr[:, 0:width] = jnp.dot(
            ft[rows, :], lg[:, first:first + width], preferred_element_type=F32
        )
        for j in range(8):
            unit = scr[j * ROWS:(j + 1) * ROWS, 0:width].astype(BF16)
            if first == 0:
                ga[j, g] = unit
            else:
                i, k = where_b(g, j)
                gb[i, k] = unit
        return carry

    lax.fori_loop(0, 8, lambda g, s: weight_part(g, s, 0, WA), 0)
    core_a = [remote(ga.at[k * 2 + co], rca.at[k], C, co) for k in (zo, zp, zm, z)]
    lax.fori_loop(0, 8, lambda g, s: weight_part(g, s, WA, WB), 0)
    core_b = [remote(gb.at[k * 2 + co], rcb.at[k], C, co) for k in (xo, xp, xm, x)]

    def add_units(dst, srcs, n):
        def step(k, carry):
            total = dst[k].astype(F32)
            for src in srcs:
                total = total + src[k].astype(F32)
            dst[k] = total.astype(BF16)
            return carry
        lax.fori_loop(0, n, step, 0)

    def hop_one(buf, rc, core, one, two, axis, opp, nxt, prv):
        core[0].wait_recv()
        add_units(buf.at[opp * 2 + c], [rc.at[opp]], 8)
        up = remote(buf.at[opp * 2 + c, 0:4], one.at[0], axis, nxt)
        down = remote(buf.at[opp * 2 + c, 4:8], one.at[1], axis, prv)
        core[1].wait_recv()
        add_units(buf.at[nxt * 2 + c], [rc.at[nxt]], 8)
        near_up = remote(buf.at[nxt * 2 + c, 4:8], two.at[0, 4:8], axis, nxt)
        core[2].wait_recv()
        add_units(buf.at[prv * 2 + c], [rc.at[prv]], 8)
        near_down = remote(buf.at[prv * 2 + c, 0:4], two.at[1, 0:4], axis, prv)
        return up, down, near_up, near_down

    def hop_two(buf, one, two, hops, axis, nxt, prv):
        hops[0].wait_recv()
        add_units(buf.at[nxt * 2 + c, 0:4], [one.at[0]], 4)
        up = remote(buf.at[nxt * 2 + c, 0:4], two.at[0, 0:4], axis, nxt)
        hops[1].wait_recv()
        add_units(buf.at[prv * 2 + c, 4:8], [one.at[1]], 4)
        down = remote(buf.at[prv * 2 + c, 4:8], two.at[1, 4:8], axis, prv)
        return up, down, hops[2], hops[3]

    hops_a = hop_one(ga, rca, core_a, r1a, r2a, Z, zo, zp, zm)
    hops_b = hop_one(gb, rcb, core_b, r1b, r2b, X, xo, xp, xm)

    bias_c.wait_recv()
    bz[z] = bc[0] + bc[1]
    bias_z = [remote(bz.at[z], bz.at[z], Z, k) for k in (zp, zm, zo)]

    core_a[3].wait_recv()
    add_units(ga.at[za], [rca.at[z]], 8)
    core_b[3].wait_recv()
    add_units(gb.at[xb], [rcb.at[x]], 8)
    hops_a = hop_two(ga, r1a, r2a, hops_a, Z, zp, zm)
    hops_b = hop_two(gb, r1b, r2b, hops_b, X, xp, xm)

    own_part = f.at[0:512]
    feature_half(0, own_part, 0)
    feature_half(0, own_part, 1)

    for copy in bias_z:
        copy.wait_recv()
    bx[x] = (bz[0] + bz[1]) + (bz[2] + bz[3])
    bias_x = [remote(bx.at[x], bx.at[x], X, k) for k in (xp, xm, xo)]

    for copy in hops_a:
        copy.wait_recv()
    add_units(ga.at[za], [r2a.at[0], r2a.at[1]], 8)
    t1p = remote(ga.at[za, 2 * xo], q1a.at[0], X, xp)
    t1m = remote(ga.at[za, 2 * xo + 1], q1a.at[1], X, xm)
    t2p = remote(ga.at[za, 2 * xp + 1], q2a.at[0, 1], X, xp)
    t2m = remote(ga.at[za, 2 * xm], q2a.at[1, 0], X, xm)

    for copy in hops_b:
        copy.wait_recv()
    add_units(gb.at[xb], [r2b.at[0], r2b.at[1]], 8)
    far = gb.at[xb, pl.ds(4 * yo, 4)]
    u0 = remote(far, ryb, Y, yo)

    t1p.wait_recv()
    ga[za, 2 * xp] = (ga[za, 2 * xp].astype(F32) + q1a[0].astype(F32)).astype(BF16)
    t3p = remote(ga.at[za, 2 * xp], q2a.at[0, 0], X, xp)
    t1m.wait_recv()
    ga[za, 2 * xm + 1] = (ga[za, 2 * xm + 1].astype(F32) + q1a[1].astype(F32)).astype(BF16)
    t3m = remote(ga.at[za, 2 * xm + 1], q2a.at[1, 1], X, xm)

    u0.wait_recv()
    add_units(gb.at[xb, pl.ds(4 * y, 4)], [ryb], 4)
    near, up, down = y * 4 + zo, y * 4 + zp, y * 4 + zm
    u1p = remote(gb.at[xb, near, :, 0:512], q1b.at[:, 0:512], Z, zp)
    u1m = remote(gb.at[xb, near, :, 512:WB], q1b.at[:, 512:WB], Z, zm)
    u2p = remote(gb.at[xb, up, :, 512:WB], q2b.at[0, :, 512:WB], Z, zp)
    u2m = remote(gb.at[xb, down, :, 0:512], q2b.at[1, :, 0:512], Z, zm)

    for copy in bias_x:
        copy.wait_recv()
    by[y] = (bx[0] + bx[1]) + (bx[2] + bx[3])
    bias_y = remote(by.at[y], by.at[y], Y, yo)

    for copy in (t2p, t2m, t3p, t3m):
        copy.wait_recv()
    add_units(ga.at[za, pair], [q2a.at[0], q2a.at[1]], 2)
    v0 = remote(ga.at[za, 2 * x + yo], rya, Y, yo)

    u1p.wait_recv()
    gb[xb, up, :, 0:512] = (
        gb[xb, up, :, 0:512].astype(F32) + q1b[:, 0:512].astype(F32)
    ).astype(BF16)
    u3p = remote(gb.at[xb, up, :, 0:512], q2b.at[0, :, 0:512], Z, zp)
    u1m.wait_recv()
    gb[xb, down, :, 512:WB] = (
        gb[xb, down, :, 512:WB].astype(F32) + q1b[:, 512:WB].astype(F32)
    ).astype(BF16)
    u3m = remote(gb.at[xb, down, :, 512:WB], q2b.at[1, :, 512:WB], Z, zm)

    for k, copy in enumerate(back):
        copy.wait_recv()

    def last_add(r, carry):
        at = pl.ds(pl.multiple_of(r * 32, 32), 32)
        f[at, :] = (f[at, :].astype(F32) + frecv[at, :].astype(F32)).astype(BF16)
        return carry

    lax.fori_loop(0, 16, last_add, 0)
    for b in range(2):
        outs.append(local(f.at[b * IMG:(b + 1) * IMG, 0:DINO], dino_grad.at[b, 0]))
        outs.append(local(f.at[b * IMG:(b + 1) * IMG, DINO:FEAT], siglip_grad.at[b, 0]))

    v0.wait_recv()
    wout[:, 0:WA] = ga[za, ua].astype(F32) + rya[...].astype(F32)
    for copy in (u2p, u2m, u3p, u3m):
        copy.wait_recv()
    wout[:, WA:FEAT] = (
        gb[xb, ub].astype(F32) + q2b[0].astype(F32) + q2b[1].astype(F32)
    )
    outs.append(local(wout, wgrad))
    bias_y.wait_recv()
    bsum[...] = by[0] + by[1]
    outs.append(local(bsum, bgrad))
    for copy in outs:
        copy.wait()
    wait_sends()


def shards(dino_feats, siglip_feats, proj_weight, proj_bias, hidden_grad):
    vm = pltpu.VMEM
    unit_a, unit_b = (ROWS, WA), (ROWS, WB)
    scratch = [
        vm((8, 8, *unit_a), BF16), vm((8, 8, *unit_b), BF16),
        vm((FEAT, FEAT), BF16), vm((1024, FEAT), BF16), vm((FEAT, 1024), BF16),
        vm((1024, FEAT), BF16), vm((512, FEAT), BF16), vm((512, FEAT), BF16),
        vm((512, FEAT), BF16),
        vm((4, 8, *unit_a), BF16), vm((4, 8, *unit_b), BF16),
        vm((2, 4, *unit_a), BF16), vm((2, 8, *unit_a), BF16),
        vm((2, 4, *unit_b), BF16), vm((2, 8, *unit_b), BF16),
        vm((2, *unit_a), BF16), vm((2, 2, *unit_a), BF16), vm(unit_a, BF16),
        vm(unit_b, BF16), vm((2, *unit_b), BF16), vm((4, *unit_b), BF16),
        vm((GROUP, WB), F32), vm((512, 512), F32), vm((ROWS, FEAT), F32),
        vm((1, FEAT), F32), vm((1, FEAT), F32),
        vm((2, 1, FEAT), F32), vm((4, 1, FEAT), F32), vm((4, 1, FEAT), F32),
        vm((2, 1, FEAT), F32),
        pltpu.SemaphoreType.DMA((COPIES,)), pltpu.SemaphoreType.DMA((COPIES,)),
        pltpu.SemaphoreType.DMA((LOCALS,)),
    ]
    anywhere = pl.BlockSpec(memory_space=pl.ANY)
    hidden, wgrad, bgrad, dino_grad, siglip_grad = pl.pallas_call(
        kernel,
        out_shape=(
            jax.ShapeDtypeStruct(hidden_grad.shape, BF16),
            jax.ShapeDtypeStruct((ROWS, FEAT), F32),
            jax.ShapeDtypeStruct((1, FEAT), F32),
            jax.ShapeDtypeStruct(dino_feats.shape, BF16),
            jax.ShapeDtypeStruct(siglip_feats.shape, BF16),
        ),
        in_specs=[anywhere] * 5,
        out_specs=[anywhere] * 5,
        scratch_shapes=scratch,
        compiler_params=pltpu.CompilerParams(
            collective_id=0, has_side_effects=True, vmem_limit_bytes=62 * 2**20
        ),
        cost_estimate=pl.CostEstimate(
            flops=6 * 1024 * FEAT * FEAT, bytes_accessed=20 * 2**20, transcendentals=4 * 2**20
        ),
    )(dino_feats, siglip_feats, proj_weight, proj_bias.reshape(1, FEAT), hidden_grad)
    return hidden, wgrad, bgrad.reshape(FEAT), dino_grad, siglip_grad


def solution(mesh):
    finer = Mesh(mesh.devices.reshape(mesh.shape["enc"], 4, 2, 4, 2), (E, *FSDP))
    in_specs = (
        P(FSDP, E, None, None), P(FSDP, E, None, None), P(FSDP, E), P(E), P(FSDP, None, E),
    )
    out_specs = (
        P(FSDP, None, E), P(FSDP, E), P(E), P(FSDP, E, None, None), P(FSDP, E, None, None),
    )
    return jax.shard_map(
        shards, mesh=finer, in_specs=in_specs, out_specs=out_specs, check_vma=False
    )
```

time: 691 us -> 197 us (0.29)
  waiting for transfers between devices: 526 us -> 0 us
  Pallas kernels: 0 us -> 186 us
  matrix products: 73.1 us -> 0 us
  local copies, waits for them, and re-layouts: 49 us -> 8.86 us
  other arithmetic: 16.2 us -> 1.33 us
  between operations: 13.8 us -> 0.64 us
  starting transfers between devices: 11.8 us -> 0 us
    unnamed x5 -> x0, waiting for transfers between devices: 258 us -> none
    pallas_call x0 -> x1, Pallas kernels: none -> 186 us  [shards(): pl.pallas_call(kernel, out_shape=(jax.ShapeDtypeStruct(hidden_grad.shape,...]
    all_gather x2 -> x0, waiting for transfers between devices: 144 us -> none  [the longest x1 80 us: shards(): whole_weight = lax.all_gather(proj_weight, FSDP, axis=0, tiled=True)]
    all_to_all x1 -> x0, waiting for transfers between devices: 95.2 us -> none  [sent_to_all(): lax.all_to_all(jnp.broadcast_to(array[None], (length, *array.shape)), axi...]
    dot_general x3 -> x0, matrix products: 73.1 us -> none  [the longest x1 42.3 us: shards(): preact = jnp.dot(feats, whole_weight, preferred_element_type=jnp.float32)]
    reduce_scatter x1 -> x0, waiting for transfers between devices: 28.9 us -> none  [sum_by_chip_2(): pieces = lax.psum_scatter(pieces, core, scatter_dimension=0, tiled=True)]
    unnamed x10, local copies, waits for them, and re-layouts: 19.8 us -> 7.55 us
    convert_element_type x2 -> x0, other arithmetic: 12.1 us -> none  [the longest x1 9.26 us: shards(): hidden_out = activated.astype(jnp.bfloat16).reshape(hidden_grad.shape)]
  transfers between devices with their start and end apart: 6 -> 0, of which waited for: 5 -> 0; matrix products, arithmetic and copies ran while one was open for 7% -> 0% of each run, Pallas kernels for 0% -> 0%
where the time goes in v1:
time: 197 us; the launch traced here: 196 us
  Pallas kernels  186 us (94%)
  local copies, waits for them, and re-layouts  8.86 us (4%)
    pallas_call x1, Pallas kernels, shards(): pl.pallas_call(kernel, out_shape=(jax.ShapeDtypeStruct(hidden_grad.shape,...  186 us
    unnamed x10, local copies, waits for them, and re-layouts  7.55 us

profile of v1, /device:TPU:0, one launch (start us, length us, event | category | flops | bytes accessed | tf_op | source)
XLA Modules:
  0.0 196.5 jit_solution(16540773028396933262)
XLA Ops:
  0.6 1.3 reshape.16.bias_in
  1.9 185.6 %shard_map.92 = (bf16[2,512,2176]{2,1,0:T(8,128)(2,1)}, f32[34,2176]{1,0:T(8,128)}, f32[1,2176]{1,0:T(1,128)}, bf16[2,1,256,1024]{3,2,1,0:T(8,128)(2,1)}, bf16[2,1,256,1152]{3,2,1,0:T(8,128)(2,1)}) custom-call(bf16[2,1,256,1024]{3,2,1,0:T(8,128)(2,1)} %dino.1, bf16[2,1,256,1152]{3,2,1,0:T(8,128)(2,1)} %siglip.1, bf16[34,2176]{1,0:T(8,128)(2,1)} %w.1, ...), custom_call_target="tpu_custom_call" | custom-call | flops 29091692544 | bytes 20971520 | tf_op jit(solution)/shard_map/pallas_call | solution.py:436
  187.6 1.3 reduce
  188.9 0.0 copy-start.2
  188.9 0.0 copy-start.1
  188.9 0.0 copy-start
  188.9 4.8 %copy.14 = bf16[2,512,2176]{2,1,0:T(8,128)(2,1)} copy(bf16[2,512,2176]{2,1,0:T(8,128)(2,1)} %get-tuple-element.20) | data formatting | bytes 8912896
  193.8 0.0 copy-done.2
  193.8 0.7 copy.15
  194.5 0.0 copy-done.1
  194.5 1.0 copy.16
  195.5 0.0 copy-done
  195.5 1.0 copy.17
Async XLA Ops:
  188.9 4.8 %copy-start.2 = (f32[34,2176]{1,0:T(8,128)S(1)}, f32[34,2176]{1,0:T(8,128)}, u32[]{:S(2)}) copy-start(f32[34,2176]{1,0:T(8,128)} %get-tuple-element.21) | copy-start | bytes 887812
  188.9 5.6 %copy-start.1 = (bf16[2,1,256,1024]{3,2,1,0:T(8,128)(2,1)S(1)}, bf16[2,1,256,1024]{3,2,1,0:T(8,128)(2,1)}, u32[]{:S(2)}) copy-start(bf16[2,1,256,1024]{3,2,1,0:T(8,128)(2,1)} %get-tuple-element.23) | copy-start | bytes 3145732
  188.9 6.5 %copy-start = (bf16[2,1,256,1152]{3,2,1,0:T(8,128)(2,1)S(1)}, bf16[2,1,256,1152]{3,2,1,0:T(8,128)(2,1)}, u32[]{:S(2)}) copy-start(bf16[2,1,256,1152]{3,2,1,0:T(8,128)(2,1)} %get-tuple-element.24) | copy-start | bytes 3538948

commit v2 on v1

v2 whole, which is shorter than its diff:
```python
import jax
import jax.numpy as jnp
from jax import lax
from jax.experimental import pallas as pl
from jax.experimental.pallas import tpu as pltpu
from jax.sharding import Mesh
from jax.sharding import PartitionSpec as P

E, X, Y, Z, C = "enc", "fsdp_0", "fsdp_1", "fsdp_2", "fsdp_3"
FSDP = (X, Y, Z, C)
DINO = 1024
SIG = 1152
FEAT = 2176
IMG = 256
ROWS = 34
WA = 1024
WB = 1152
GROUP = 8 * ROWS
F32 = jnp.float32
BF16 = jnp.bfloat16
CUT_A = (slice(0, 512), slice(512, WA))
CUT_B = (slice(0, 640), slice(640, WB))
COPIES = 136
LOCALS = 24


def kernel(
    dino, siglip, w, bias_in, hg,
    hidden, wgrad, bgrad, dino_grad, siglip_grad,
    ga, gb, wd, f, ft, lg, hid, fsend, frecv,
    rca, rcb, r1a, r2a, r1b, r2b, q1a, q2a, rya, q1b, q2b, ryb,
    scr, pre, wout, bias, bsum, bc, bz, bx, by, flat_in, flat_out,
    ssem, rsem, lsem,
):
    e, x, y, z, c = (lax.axis_index(n) for n in (E, X, Y, Z, C))
    xp, xm, xo = (lax.rem(x + k, 4) for k in (1, 3, 2))
    zp, zm, zo = (lax.rem(z + k, 4) for k in (1, 3, 2))
    yo, co, eo = 1 - y, 1 - c, 1 - e
    za, ua = z * 2 + c, x * 2 + y
    xb, ub = x * 2 + c, z * 2 + y

    counts = {"remote": 0, "local": 0}
    sends = []

    def remote(src, dst, axis, to):
        i = counts["remote"]
        counts["remote"] += 1
        copy = pltpu.make_async_remote_copy(
            src_ref=src, dst_ref=dst, send_sem=ssem.at[i], recv_sem=rsem.at[i],
            device_id={axis: to}, device_id_type=pl.DeviceIdType.MESH,
        )
        copy.start()
        sends.append(copy)
        return copy

    def local(src, dst):
        i = counts["local"]
        counts["local"] += 1
        copy = pltpu.make_async_copy(src, dst, lsem.at[i])
        copy.start()
        return copy

    def wait_sends():
        for copy in sends:
            copy.wait_send()
        sends.clear()

    own_w = [local(w.at[:, 0:WA], ga.at[za, ua]), local(w.at[:, WA:FEAT], gb.at[xb, ub])]
    own_f = []
    for b in range(2):
        own_f.append(local(dino.at[b, 0], f.at[b * IMG:(b + 1) * IMG, 0:DINO]))
        own_f.append(local(siglip.at[b, 0], f.at[b * IMG:(b + 1) * IMG, DINO:FEAT]))
    own_bias = local(bias_in, flat_in)

    barrier = pltpu.get_barrier_semaphore()
    peers = [(E, eo), (C, co), (Y, yo)]
    peers += [(X, k) for k in (xp, xm, xo)] + [(Z, k) for k in (zp, zm, zo)]
    for axis, to in peers:
        pl.semaphore_signal(
            barrier, inc=1, device_id={axis: to}, device_id_type=pl.DeviceIdType.MESH
        )
    pl.semaphore_wait(barrier, len(peers))

    for copy in own_w:
        copy.wait()
    def across(buf, block, unit):
        return remote(buf.at[block, unit], buf.at[block, unit], Y, yo)

    def near_pair(buf, block, me, axis, nxt, prv):
        pair = buf.at[block, pl.ds(2 * me, 2)]
        return remote(pair, pair, axis, nxt), remote(pair, pair, axis, prv)

    def far_pair(buf, block, hops, axis, nxt, prv):
        hops[0].wait_recv()
        unit = buf.at[block, 2 * prv]
        up = remote(unit, unit, axis, nxt)
        hops[1].wait_recv()
        unit = buf.at[block, 2 * nxt + 1]
        return up, remote(unit, unit, axis, prv)

    def near_block(buf, cols, me, axis, nxt, prv, shared):
        block = buf.at[me * 2 + c, :, :, cols]
        up, down = remote(block, block, axis, nxt), remote(block, block, axis, prv)
        shared.append(remote(block, block, C, co))
        return up, down

    def far_block(buf, cols, hops, axis, nxt, prv, shared):
        hops[0].wait_recv()
        block = buf.at[prv * 2 + c, :, :, cols]
        half = buf.at[prv * 2 + c, 0:4, :, cols]
        up = remote(half, half, axis, nxt)
        shared.append(remote(block, block, C, co))
        hops[1].wait_recv()
        block = buf.at[nxt * 2 + c, :, :, cols]
        half = buf.at[nxt * 2 + c, 4:8, :, cols]
        down = remote(half, half, axis, prv)
        shared.append(remote(block, block, C, co))
        return up, down

    def last_block(buf, cols, hops, opp, shared):
        for k, hop in enumerate(hops):
            hop.wait_recv()
            half = buf.at[opp * 2 + c, 4 * k:4 * k + 4, :, cols]
            shared.append(remote(half, half, C, co))

    def arrived(shared):
        for copy in shared:
            copy.wait_recv()

    shared = ([], [])
    across_a = across(ga, za, ua)
    across_b = across(gb, xb, ub)
    far_f = []
    for b in range(2):
        rows = slice(2 * IMG + b * IMG, 2 * IMG + (b + 1) * IMG)
        far_f.append(remote(dino.at[b, 0], f.at[rows, 0:DINO], E, eo))
        far_f.append(remote(siglip.at[b, 0], f.at[rows, DINO:FEAT], E, eo))
    del sends[-4:]
    own_hg = []
    for i, image in enumerate((e, eo)):
        for b in range(2):
            own_hg.append(
                local(
                    hg.at[b, pl.ds(pl.multiple_of(image * IMG, IMG), IMG)],
                    lg.at[(2 * i + b) * IMG:(2 * i + b + 1) * IMG],
                )
            )

    across_a.wait_recv()
    hops_a = near_pair(ga, za, x, X, xp, xm)
    across_b.wait_recv()
    hops_b = near_pair(gb, xb, z, Z, zp, zm)
    hops_a = far_pair(ga, za, hops_a, X, xp, xm)
    hops_b = far_pair(gb, xb, hops_b, Z, zp, zm)
    for hop in hops_a:
        hop.wait_recv()
    hops_a = near_block(ga, CUT_A[0], z, Z, zp, zm, shared[0])
    for hop in hops_b:
        hop.wait_recv()
    hops_b = near_block(gb, CUT_B[0], x, X, xp, xm, shared[0])

    def transposed(first, count):
        def step(t, carry):
            cols = pl.ds(pl.multiple_of(t * 128, 128), 128)
            ft[cols, first:first + count] = f[first:first + count, cols].T
            return carry
        lax.fori_loop(0, FEAT // 128, step, 0)

    for copy in own_f:
        copy.wait()
    transposed(0, 512)

    hops_a = far_block(ga, CUT_A[0], hops_a, Z, zp, zm, shared[0])
    then_a = near_block(ga, CUT_A[1], z, Z, zp, zm, shared[1])
    hops_b = far_block(gb, CUT_B[0], hops_b, X, xp, xm, shared[0])
    then_b = near_block(gb, CUT_B[1], x, X, xp, xm, shared[1])
    last_block(ga, CUT_A[0], hops_a, zo, shared[0])
    last_block(gb, CUT_B[0], hops_b, xo, shared[0])
    arrived(shared[0])

    def where_b(g, j):
        return (g // 2) * 2 + j % 2, (j // 2) * 2 + lax.rem(g, 2)

    def assembled(n):
        def step(g, carry):
            rows = pl.ds(pl.multiple_of(g * GROUP, 16), GROUP)
            cols = CUT_A[n]
            for j in range(8):
                scr[j * ROWS:(j + 1) * ROWS, 0:512] = ga[j, g, :, cols].astype(F32)
            wd[rows, cols] = scr[:, 0:512].astype(BF16)
            cols = CUT_B[n]
            width = cols.stop - cols.start
            for j in range(8):
                i, k = where_b(g, j)
                scr[j * ROWS:(j + 1) * ROWS, 0:width] = gb[i, k, :, cols].astype(F32)
            wd[rows, WA + cols.start:WA + cols.stop] = scr[:, 0:width].astype(BF16)
            return carry
        lax.fori_loop(0, 8, step, 0)

    assembled(0)

    bsum[...] = jnp.zeros_like(bsum)
    own_bias.wait()
    bias[...] = flat_in[...].reshape(1, FEAT)

    def forward(n, first, count):
        def tile(start, width):
            cols = pl.ds(start, width)
            pre[0:count, 0:width] = jnp.dot(
                f[first:first + count, :], wd[:, cols], preferred_element_type=F32
            )

            def rows_step(r, acc):
                at = pl.ds(pl.multiple_of(r * 32, 32), 32)
                lat = pl.ds(pl.multiple_of(first + r * 32, 32), 32)
                v = pre[at, 0:width] + bias[:, cols]
                cdf = 0.5 + 0.5 * lax.erf(v * 0.7071067811865476)
                pdf = jnp.exp(v * v * -0.5) * 0.3989422804014327
                hid[lat, cols] = (v * cdf).astype(BF16)
                grad = (lg[lat, cols].astype(F32) * (cdf + v * pdf)).astype(BF16)
                lg[lat, cols] = grad
                wide = grad.astype(F32)
                return acc + (wide[0:8] + wide[8:16] + wide[16:24] + wide[24:32])

            acc = lax.fori_loop(0, count // 32, rows_step, jnp.zeros((8, width), F32))
            bsum[:, cols] += jnp.sum(acc, axis=0, keepdims=True)

        tile(CUT_A[n].start, 512)
        tile(WA + CUT_B[n].start, CUT_B[n].stop - CUT_B[n].start)

    def hidden_out(k):
        image = e if k < 2 else eo
        return local(
            hid.at[k * IMG:(k + 1) * IMG],
            hidden.at[k % 2, pl.ds(pl.multiple_of(image * IMG, IMG), IMG)],
        )

    def feature_part(first, count, dst, start, width):
        dst[:, pl.ds(start, width)] = lax.dot_general(
            lg[first:first + count, :], wd[pl.ds(start, width), :],
            (((1,), (1,)), ((), ())), preferred_element_type=F32,
        ).astype(BF16)

    def feature_grad(first, count, dst):
        def step(t, carry):
            feature_part(first, count, dst, pl.multiple_of(t * 512, 512), 512)
            return carry
        lax.fori_loop(0, 4, step, 0)
        feature_part(first, count, dst, 2048, 128)

    def give_back(k):
        rows = slice(k * IMG, (k + 1) * IMG)
        feature_grad((2 + k) * IMG, IMG, fsend.at[rows])
        back.append(remote(fsend.at[rows], frecv.at[rows], E, eo))

    outs, back = [], []
    own_hg[0].wait()
    own_hg[1].wait()
    forward(0, 0, 2 * IMG)
    hops_a = far_block(ga, CUT_A[1], then_a, Z, zp, zm, shared[1])
    hops_b = far_block(gb, CUT_B[1], then_b, X, xp, xm, shared[1])
    far_f[0].wait_recv()
    far_f[1].wait_recv()
    own_hg[2].wait()
    forward(0, 2 * IMG, IMG)
    last_block(ga, CUT_A[1], hops_a, zo, shared[1])
    last_block(gb, CUT_B[1], hops_b, xo, shared[1])
    transposed(2 * IMG, IMG)
    arrived(shared[1])
    gathered = list(sends)
    sends.clear()
    assembled(1)
    forward(1, 2 * IMG, IMG)
    outs.append(hidden_out(2))
    give_back(0)
    forward(1, 0, 2 * IMG)
    outs.append(hidden_out(0))
    outs.append(hidden_out(1))
    far_f[2].wait_recv()
    far_f[3].wait_recv()
    own_hg[3].wait()
    forward(0, 3 * IMG, IMG)
    forward(1, 3 * IMG, IMG)
    outs.append(hidden_out(3))
    transposed(3 * IMG, IMG)
    for copy in gathered:
        copy.wait_send()
    sends.extend(far_f)

    bc[c] = bsum[...]
    bias_c = remote(bc.at[c], bc.at[c], C, co)

    def weight_part(buf, cols):
        width = cols.stop - cols.start
        at = slice(cols.start + (WA if buf is gb else 0), cols.stop + (WA if buf is gb else 0))

        def step(g, carry):
            rows = pl.ds(pl.multiple_of(g * GROUP, 16), GROUP)
            scr[:, 0:width] = jnp.dot(ft[rows, :], lg[:, at], preferred_element_type=F32)
            for j in range(8):
                i, k = where_b(g, j) if buf is gb else (j, g)
                buf[i, k, :, cols] = scr[j * ROWS:(j + 1) * ROWS, 0:width].astype(BF16)
            return carry

        lax.fori_loop(0, 8, step, 0)

    def core_part(buf, rc, cols, order):
        weight_part(buf, cols)
        return [
            remote(buf.at[k * 2 + co, :, :, cols], rc.at[k, :, :, cols], C, co) for k in order
        ]

    def add_units(dst, srcs, n):
        def step(k, carry):
            total = dst[k].astype(F32)
            for src in srcs:
                total = total + src[k].astype(F32)
            dst[k] = total.astype(BF16)
            return carry
        lax.fori_loop(0, n, step, 0)

    def hop_one(buf, rc, core, one, two, cols, axis, opp, nxt, prv):
        def block(k):
            return buf.at[k * 2 + c, :, :, cols]

        def part(ref, *at):
            return ref.at[(*at, slice(None), cols)]

        low, high = slice(0, 4), slice(4, 8)
        core[0].wait_recv()
        add_units(block(opp), [rc.at[opp, :, :, cols]], 8)
        up = remote(part(buf, opp * 2 + c, low), part(one, 0, slice(None)), axis, nxt)
        down = remote(part(buf, opp * 2 + c, high), part(one, 1, slice(None)), axis, prv)
        core[1].wait_recv()
        add_units(block(nxt), [rc.at[nxt, :, :, cols]], 8)
        near_up = remote(part(buf, nxt * 2 + c, high), part(two, 0, high), axis, nxt)
        core[2].wait_recv()
        add_units(block(prv), [rc.at[prv, :, :, cols]], 8)
        near_down = remote(part(buf, prv * 2 + c, low), part(two, 1, low), axis, prv)
        return up, down, near_up, near_down

    def hop_two(buf, one, two, cols, hops, axis, nxt, prv):
        hops[0].wait_recv()
        half = buf.at[nxt * 2 + c, 0:4, :, cols]
        add_units(half, [one.at[0, :, :, cols]], 4)
        up = remote(half, two.at[0, 0:4, :, cols], axis, nxt)
        hops[1].wait_recv()
        half = buf.at[prv * 2 + c, 4:8, :, cols]
        add_units(half, [one.at[1, :, :, cols]], 4)
        down = remote(half, two.at[1, 4:8, :, cols], axis, prv)
        return up, down, hops[2], hops[3]

    def own_block(buf, rc, core, cols, me):
        core[3].wait_recv()
        add_units(buf.at[me * 2 + c, :, :, cols], [rc.at[me, :, :, cols]], 8)

    def hop_last(buf, two, cols, hops, me):
        for copy in hops:
            copy.wait_recv()
        add_units(
            buf.at[me * 2 + c, :, :, cols],
            [two.at[0, :, :, cols], two.at[1, :, :, cols]], 8,
        )

    order_a, order_b = (zo, zp, zm, z), (xo, xp, xm, x)
    along_a, along_b = (Z, zo, zp, zm), (X, xo, xp, xm)
    core_a0 = core_part(ga, rca, CUT_A[0], order_a)
    core_b0 = core_part(gb, rcb, CUT_B[0], order_b)
    hops_a0 = hop_one(ga, rca, core_a0, r1a, r2a, CUT_A[0], *along_a)
    core_a1 = core_part(ga, rca, CUT_A[1], order_a)
    hops_b0 = hop_one(gb, rcb, core_b0, r1b, r2b, CUT_B[0], *along_b)
    give_back(1)
    core_b1 = core_part(gb, rcb, CUT_B[1], order_b)
    hops_a0 = hop_two(ga, r1a, r2a, CUT_A[0], hops_a0, Z, zp, zm)
    hops_a1 = hop_one(ga, rca, core_a1, r1a, r2a, CUT_A[1], *along_a)
    hops_b0 = hop_two(gb, r1b, r2b, CUT_B[0], hops_b0, X, xp, xm)
    hops_b1 = hop_one(gb, rcb, core_b1, r1b, r2b, CUT_B[1], *along_b)

    def pair_one(buf, block, q1, q2, cols, axis, opp, nxt, prv):
        def unit(k):
            return buf.at[block, k, :, cols]

        up = remote(unit(2 * opp), q1.at[0, :, cols], axis, nxt)
        down = remote(unit(2 * opp + 1), q1.at[1, :, cols], axis, prv)
        near_up = remote(unit(2 * nxt + 1), q2.at[0, 1, :, cols], axis, nxt)
        near_down = remote(unit(2 * prv), q2.at[1, 0, :, cols], axis, prv)
        return up, down, near_up, near_down

    def pair_two(buf, block, q1, q2, cols, hops, axis, nxt, prv):
        def add(k, src):
            total = buf[block, k, :, cols].astype(F32) + src[:, cols].astype(F32)
            buf[block, k, :, cols] = total.astype(BF16)
            return buf.at[block, k, :, cols]

        hops[0].wait_recv()
        up = remote(add(2 * nxt, q1.at[0]), q2.at[0, 0, :, cols], axis, nxt)
        hops[1].wait_recv()
        down = remote(add(2 * prv + 1, q1.at[1]), q2.at[1, 1, :, cols], axis, prv)
        return up, down, hops[2], hops[3]

    def pair_last(buf, block, q2, cols, hops, me):
        for copy in hops:
            copy.wait_recv()
        add_units(
            buf.at[block, pl.ds(2 * me, 2), :, cols],
            [q2.at[0, :, :, cols], q2.at[1, :, :, cols]], 2,
        )

    def returned(k):
        back[k].wait_recv()

        def step(r, carry):
            at = pl.ds(pl.multiple_of(k * IMG + r * 32, 32), 32)
            f[at, :] = (f[at, :].astype(F32) + frecv[at, :].astype(F32)).astype(BF16)
            return carry

        lax.fori_loop(0, 8, step, 0)
        outs.append(local(f.at[k * IMG:(k + 1) * IMG, 0:DINO], dino_grad.at[k, 0]))
        outs.append(local(f.at[k * IMG:(k + 1) * IMG, DINO:FEAT], siglip_grad.at[k, 0]))

    bias_c.wait_recv()
    bz[z] = bc[0] + bc[1]
    bias_z = [remote(bz.at[z], bz.at[z], Z, k) for k in (zp, zm, zo)]

    pair_a, pair_b = (za, q1a, q2a), (xb, q1b, q2b)
    own_block(ga, rca, core_a0, CUT_A[0], z)
    hop_last(ga, r2a, CUT_A[0], hops_a0, z)
    hops_a0 = pair_one(ga, *pair_a, CUT_A[0], X, xo, xp, xm)
    own_block(gb, rcb, core_b0, CUT_B[0], x)
    hop_last(gb, r2b, CUT_B[0], hops_b0, x)
    hops_b0 = pair_one(gb, *pair_b, CUT_B[0], Z, zo, zp, zm)
    hops_a1 = hop_two(ga, r1a, r2a, CUT_A[1], hops_a1, Z, zp, zm)
    hops_b1 = hop_two(gb, r1b, r2b, CUT_B[1], hops_b1, X, xp, xm)
    own_block(ga, rca, core_a1, CUT_A[1], z)
    own_block(gb, rcb, core_b1, CUT_B[1], x)
    hops_a0 = pair_two(ga, *pair_a, CUT_A[0], hops_a0, X, xp, xm)
    hops_b0 = pair_two(gb, *pair_b, CUT_B[0], hops_b0, Z, zp, zm)

    feature_grad(0, 2 * IMG, f.at[0:2 * IMG])

    hop_last(ga, r2a, CUT_A[1], hops_a1, z)
    hops_a1 = pair_one(ga, *pair_a, CUT_A[1], X, xo, xp, xm)
    hop_last(gb, r2b, CUT_B[1], hops_b1, x)
    hops_b1 = pair_one(gb, *pair_b, CUT_B[1], Z, zo, zp, zm)

    for copy in bias_z:
        copy.wait_recv()
    bx[x] = (bz[0] + bz[1]) + (bz[2] + bz[3])
    bias_x = [remote(bx.at[x], bx.at[x], X, k) for k in (xp, xm, xo)]

    returned(0)
    pair_last(ga, za, q2a, CUT_A[0], hops_a0, x)
    pair_last(gb, xb, q2b, CUT_B[0], hops_b0, z)
    hops_a1 = pair_two(ga, *pair_a, CUT_A[1], hops_a1, X, xp, xm)
    hops_b1 = pair_two(gb, *pair_b, CUT_B[1], hops_b1, Z, zp, zm)
    for copy in bias_x:
        copy.wait_recv()
    by[y] = (bx[0] + bx[1]) + (bx[2] + bx[3])
    bias_y = remote(by.at[y], by.at[y], Y, yo)
    pair_last(ga, za, q2a, CUT_A[1], hops_a1, x)
    end_a = remote(ga.at[za, 2 * x + yo], rya, Y, yo)
    pair_last(gb, xb, q2b, CUT_B[1], hops_b1, z)
    end_b = remote(gb.at[xb, 2 * z + yo], ryb, Y, yo)
    returned(1)

    end_a.wait_recv()
    wout[:, 0:WA] = ga[za, ua].astype(F32) + rya[...].astype(F32)
    end_b.wait_recv()
    wout[:, WA:FEAT] = gb[xb, ub].astype(F32) + ryb[...].astype(F32)
    outs.append(local(wout, wgrad))
    bias_y.wait_recv()
    flat_out[...] = (by[0] + by[1]).reshape(FEAT)
    outs.append(local(flat_out, bgrad))
    for copy in outs:
        copy.wait()
    wait_sends()


def handed_on(*refs):
    srcs, dsts, held, sem = refs[:5], refs[5:10], refs[10:15], refs[15]
    pieces = [(0, (b, slice(r * 128, (r + 1) * 128))) for b in range(2) for r in range(4)]
    pieces += [(k, b) for k in (3, 4) for b in range(2)] + [(1, ...), (2, ...)]

    def part(ref, at):
        return ref if at is ... else ref.at[at]

    ins, outs = [], []
    for n, (k, at) in enumerate(pieces):
        ins.append(pltpu.make_async_copy(part(srcs[k], at), part(held[k], at), sem.at[0, n]))
        outs.append(pltpu.make_async_copy(part(held[k], at), part(dsts[k], at), sem.at[1, n]))
    for copy in ins:
        copy.start()
    for fetched, copy in zip(ins, outs):
        fetched.wait()
        copy.start()
    for copy in outs:
        copy.wait()


def shards(dino_feats, siglip_feats, proj_weight, proj_bias, hidden_grad):
    vm = pltpu.VMEM
    unit_a, unit_b = (ROWS, WA), (ROWS, WB)
    scratch = [
        vm((8, 8, *unit_a), BF16), vm((8, 8, *unit_b), BF16),
        vm((FEAT, FEAT), BF16), vm((1024, FEAT), BF16), vm((FEAT, 1024), BF16),
        vm((1024, FEAT), BF16), vm((1024, FEAT), BF16), vm((512, FEAT), BF16),
        vm((512, FEAT), BF16),
        vm((4, 8, *unit_a), BF16), vm((4, 8, *unit_b), BF16),
        vm((2, 4, *unit_a), BF16), vm((2, 8, *unit_a), BF16),
        vm((2, 4, *unit_b), BF16), vm((2, 8, *unit_b), BF16),
        vm((2, *unit_a), BF16), vm((2, 2, *unit_a), BF16), vm(unit_a, BF16),
        vm((2, *unit_b), BF16), vm((2, 2, *unit_b), BF16), vm(unit_b, BF16),
        vm((GROUP, WB), F32), vm((512, 640), F32), vm((ROWS, FEAT), F32),
        vm((1, FEAT), F32), vm((1, FEAT), F32),
        vm((2, 1, FEAT), F32), vm((4, 1, FEAT), F32), vm((4, 1, FEAT), F32),
        vm((2, 1, FEAT), F32), vm((FEAT,), F32), vm((FEAT,), F32),
        pltpu.SemaphoreType.DMA((COPIES,)), pltpu.SemaphoreType.DMA((COPIES,)),
        pltpu.SemaphoreType.DMA((LOCALS,)),
    ]
    anywhere = pl.BlockSpec(memory_space=pl.ANY)
    results = pl.pallas_call(
        kernel,
        out_shape=(
            jax.ShapeDtypeStruct(hidden_grad.shape, BF16),
            jax.ShapeDtypeStruct((ROWS, FEAT), F32),
            jax.ShapeDtypeStruct((FEAT,), F32),
            jax.ShapeDtypeStruct(dino_feats.shape, BF16),
            jax.ShapeDtypeStruct(siglip_feats.shape, BF16),
        ),
        in_specs=[anywhere] * 5,
        out_specs=[anywhere] * 5,
        scratch_shapes=scratch,
        compiler_params=pltpu.CompilerParams(
            collective_id=0, has_side_effects=True, vmem_limit_bytes=62 * 2**20
        ),
        cost_estimate=pl.CostEstimate(
            flops=6 * 1024 * FEAT * FEAT, bytes_accessed=20 * 2**20, transcendentals=4 * 2**20
        ),
    )(dino_feats, siglip_feats, proj_weight, proj_bias, hidden_grad)
    return pl.pallas_call(
        handed_on,
        out_shape=tuple(jax.ShapeDtypeStruct(r.shape, r.dtype) for r in results),
        in_specs=[anywhere] * 5,
        out_specs=[anywhere] * 5,
        scratch_shapes=[vm(r.shape, r.dtype) for r in results] + [pltpu.SemaphoreType.DMA((2, 14))],
        cost_estimate=pl.CostEstimate(flops=0, bytes_accessed=14 * 2**20, transcendentals=0),
    )(*results)


def solution(mesh):
    finer = Mesh(mesh.devices.reshape(mesh.shape["enc"], 4, 2, 4, 2), (E, *FSDP))
    in_specs = (
        P(FSDP, E, None, None), P(FSDP, E, None, None), P(FSDP, E), P(E), P(FSDP, None, E),
    )
    out_specs = (
        P(FSDP, None, E), P(FSDP, E), P(E), P(FSDP, E, None, None), P(FSDP, E, None, None),
    )
    return jax.shard_map(
        shards, mesh=finer, in_specs=in_specs, out_specs=out_specs, check_vma=False
    )
```

time: 197 us -> 140 us (0.71)
  Pallas kernels: 186 us -> 139 us
  local copies, waits for them, and re-layouts: 8.86 us -> 0 us
    pallas_call x1, Pallas kernels: 186 us -> 133 us  [shards(): pl.pallas_call(kernel, out_shape=(jax.ShapeDtypeStruct(hidden_grad.shape,...]
    unnamed x10 -> x0, local copies, waits for them, and re-layouts: 7.55 us -> none
    pallas_call x0 -> x1, Pallas kernels: none -> 5.83 us  [shards(): pl.pallas_call(handed_on, out_shape=tuple((jax.ShapeDtypeStruct(r.shape,...]
where the time goes in v2:
time: 140 us
  Pallas kernels  139 us (99%)
    pallas_call x1, Pallas kernels, shards(): pl.pallas_call(kernel, out_shape=(jax.ShapeDtypeStruct(hidden_grad.shape,...  133 us
    pallas_call x1, Pallas kernels, shards(): pl.pallas_call(handed_on, out_shape=tuple((jax.ShapeDtypeStruct(r.shape,...  5.83 us

profile of v2, /device:TPU:0, one launch (start us, length us, event | category | flops | bytes accessed | tf_op | source)
XLA Modules:
  0.0 139.5 jit_solution(6422419709276817321)
XLA Ops:
  0.6 132.9 %shard_map.92 = (bf16[2,512,2176]{2,1,0:T(8,128)(2,1)}, f32[34,2176]{1,0:T(8,128)}, f32[2176]{0:T(1024)}, bf16[2,1,256,1024]{3,2,1,0:T(8,128)(2,1)}, bf16[2,1,256,1152]{3,2,1,0:T(8,128)(2,1)}) custom-call(bf16[2,1,256,1024]{3,2,1,0:T(8,128)(2,1)} %dino.1, bf16[2,1,256,1152]{3,2,1,0:T(8,128)(2,1)} %siglip.1, bf16[34,2176]{1,0:T(8,128)(2,1)} %w.1, ...), custom_call_target="tpu_custom_call" | custom-call | flops 29091692544 | bytes 20971520 | tf_op jit(solution)/shard_map/pallas_call | solution.py:521
  133.5 5.8 %shard_map.93 = (bf16[2,512,2176]{2,1,0:T(8,128)(2,1)}, f32[34,2176]{1,0:T(8,128)}, f32[2176]{0:T(1024)}, bf16[2,1,256,1024]{3,2,1,0:T(8,128)(2,1)}, bf16[2,1,256,1152]{3,2,1,0:T(8,128)(2,1)}) custom-call(bf16[2,512,2176]{2,1,0:T(8,128)(2,1)} %get-tuple-element.10.refs_0_, f32[34,2176]{1,0:T(8,128)} %get-tuple-element.11.refs_1_, ...), custom_call_target="tpu_custom_call" | custom-call | bytes 14680064 | tf_op jit(solution)/shard_map/pallas_call | solution.py:540

commit v3 on v2

--- a/solution.py
+++ b/solution.py
@@ -29,7 +29,7 @@
     hidden, wgrad, bgrad, dino_grad, siglip_grad,
     ga, gb, wd, f, ft, lg, hid, fsend, frecv,
     rca, rcb, r1a, r2a, r1b, r2b, q1a, q2a, rya, q1b, q2b, ryb,
-    scr, pre, wout, bias, bsum, bc, bz, bx, by, flat_in, flat_out,
+    scr, pre, pre_next, wout, bias, bsum, bc, bz, bx, by, flat_in, flat_out,
     ssem, rsem, lsem,
 ):
     e, x, y, z, c = (lax.axis_index(n) for n in (E, X, Y, Z, C))
@@ -204,29 +204,43 @@
     bias[...] = flat_in[...].reshape(1, FEAT)
 
     def forward(n, first, count):
-        def tile(start, width):
-            cols = pl.ds(start, width)
-            pre[0:count, 0:width] = jnp.dot(
+        tiles = []
+        for start, stop in (
+            (CUT_A[n].start, CUT_A[n].stop), (WA + CUT_B[n].start, WA + CUT_B[n].stop)
+        ):
+            tiles += [slice(k, min(k + 256, stop)) for k in range(start, stop, 256)]
+        slots = (pre, pre_next)
+
+        def product(k):
+            cols = tiles[k]
+            slots[k % 2][0:count, 0:cols.stop - cols.start] = jnp.dot(
                 f[first:first + count, :], wd[:, cols], preferred_element_type=F32
             )
 
-            def rows_step(r, acc):
-                at = pl.ds(pl.multiple_of(r * 32, 32), 32)
-                lat = pl.ds(pl.multiple_of(first + r * 32, 32), 32)
-                v = pre[at, 0:width] + bias[:, cols]
+        def activation(k):
+            cols = tiles[k]
+            width = cols.stop - cols.start
+            slot = slots[k % 2]
+            shift = bias[:, cols]
+            acc = jnp.zeros((8, width), F32)
+            for r in range(count // 16):
+                at = slice(r * 16, (r + 1) * 16)
+                lat = slice(first + r * 16, first + (r + 1) * 16)
+                v = slot[at, 0:width] + shift
                 cdf = 0.5 + 0.5 * lax.erf(v * 0.7071067811865476)
                 pdf = jnp.exp(v * v * -0.5) * 0.3989422804014327
                 hid[lat, cols] = (v * cdf).astype(BF16)
                 grad = (lg[lat, cols].astype(F32) * (cdf + v * pdf)).astype(BF16)
                 lg[lat, cols] = grad
                 wide = grad.astype(F32)
-                return acc + (wide[0:8] + wide[8:16] + wide[16:24] + wide[24:32])
-
-            acc = lax.fori_loop(0, count // 32, rows_step, jnp.zeros((8, width), F32))
+                acc = acc + (wide[0:8] + wide[8:16])
             bsum[:, cols] += jnp.sum(acc, axis=0, keepdims=True)
 
-        tile(CUT_A[n].start, 512)
-        tile(WA + CUT_B[n].start, CUT_B[n].stop - CUT_B[n].start)
+        product(0)
+        for k in range(len(tiles)):
+            if k + 1 < len(tiles):
+                product(k + 1)
+            activation(k)
 
     def hidden_out(k):
         image = e if k < 2 else eo
@@ -364,17 +378,17 @@
 
     order_a, order_b = (zo, zp, zm, z), (xo, xp, xm, x)
     along_a, along_b = (Z, zo, zp, zm), (X, xo, xp, xm)
+    core_b0 = core_part(gb, rcb, CUT_B[0], order_b)
     core_a0 = core_part(ga, rca, CUT_A[0], order_a)
-    core_b0 = core_part(gb, rcb, CUT_B[0], order_b)
+    hops_b0 = hop_one(gb, rcb, core_b0, r1b, r2b, CUT_B[0], *along_b)
+    core_b1 = core_part(gb, rcb, CUT_B[1], order_b)
     hops_a0 = hop_one(ga, rca, core_a0, r1a, r2a, CUT_A[0], *along_a)
+    give_back(1)
+    hops_b0 = hop_two(gb, r1b, r2b, CUT_B[0], hops_b0, X, xp, xm)
+    hops_b1 = hop_one(gb, rcb, core_b1, r1b, r2b, CUT_B[1], *along_b)
     core_a1 = core_part(ga, rca, CUT_A[1], order_a)
-    hops_b0 = hop_one(gb, rcb, core_b0, r1b, r2b, CUT_B[0], *along_b)
-    give_back(1)
-    core_b1 = core_part(gb, rcb, CUT_B[1], order_b)
     hops_a0 = hop_two(ga, r1a, r2a, CUT_A[0], hops_a0, Z, zp, zm)
     hops_a1 = hop_one(ga, rca, core_a1, r1a, r2a, CUT_A[1], *along_a)
-    hops_b0 = hop_two(gb, r1b, r2b, CUT_B[0], hops_b0, X, xp, xm)
-    hops_b1 = hop_one(gb, rcb, core_b1, r1b, r2b, CUT_B[1], *along_b)
 
     def pair_one(buf, block, q1, q2, cols, axis, opp, nxt, prv):
         def unit(k):
@@ -423,44 +437,44 @@
     bias_z = [remote(bz.at[z], bz.at[z], Z, k) for k in (zp, zm, zo)]
 
     pair_a, pair_b = (za, q1a, q2a), (xb, q1b, q2b)
+    own_block(gb, rcb, core_b0, CUT_B[0], x)
     own_block(ga, rca, core_a0, CUT_A[0], z)
+    own_block(gb, rcb, core_b1, CUT_B[1], x)
+    hops_b1 = hop_two(gb, r1b, r2b, CUT_B[1], hops_b1, X, xp, xm)
+    hop_last(gb, r2b, CUT_B[0], hops_b0, x)
+    hops_b0 = pair_one(gb, *pair_b, CUT_B[0], Z, zo, zp, zm)
+    own_block(ga, rca, core_a1, CUT_A[1], z)
+    hops_a1 = hop_two(ga, r1a, r2a, CUT_A[1], hops_a1, Z, zp, zm)
     hop_last(ga, r2a, CUT_A[0], hops_a0, z)
     hops_a0 = pair_one(ga, *pair_a, CUT_A[0], X, xo, xp, xm)
-    own_block(gb, rcb, core_b0, CUT_B[0], x)
-    hop_last(gb, r2b, CUT_B[0], hops_b0, x)
-    hops_b0 = pair_one(gb, *pair_b, CUT_B[0], Z, zo, zp, zm)
-    hops_a1 = hop_two(ga, r1a, r2a, CUT_A[1], hops_a1, Z, zp, zm)
-    hops_b1 = hop_two(gb, r1b, r2b, CUT_B[1], hops_b1, X, xp, xm)
-    own_block(ga, rca, core_a1, CUT_A[1], z)
-    own_block(gb, rcb, core_b1, CUT_B[1], x)
-    hops_a0 = pair_two(ga, *pair_a, CUT_A[0], hops_a0, X, xp, xm)
-    hops_b0 = pair_two(gb, *pair_b, CUT_B[0], hops_b0, Z, zp, zm)
 
     feature_grad(0, 2 * IMG, f.at[0:2 * IMG])
 
+    hop_last(gb, r2b, CUT_B[1], hops_b1, x)
+    hops_b1 = pair_one(gb, *pair_b, CUT_B[1], Z, zo, zp, zm)
     hop_last(ga, r2a, CUT_A[1], hops_a1, z)
     hops_a1 = pair_one(ga, *pair_a, CUT_A[1], X, xo, xp, xm)
-    hop_last(gb, r2b, CUT_B[1], hops_b1, x)
-    hops_b1 = pair_one(gb, *pair_b, CUT_B[1], Z, zo, zp, zm)
+    hops_b0 = pair_two(gb, *pair_b, CUT_B[0], hops_b0, Z, zp, zm)
+    hops_a0 = pair_two(ga, *pair_a, CUT_A[0], hops_a0, X, xp, xm)
 
     for copy in bias_z:
         copy.wait_recv()
     bx[x] = (bz[0] + bz[1]) + (bz[2] + bz[3])
     bias_x = [remote(bx.at[x], bx.at[x], X, k) for k in (xp, xm, xo)]
 
+    hops_b1 = pair_two(gb, *pair_b, CUT_B[1], hops_b1, Z, zp, zm)
+    hops_a1 = pair_two(ga, *pair_a, CUT_A[1], hops_a1, X, xp, xm)
     returned(0)
-    pair_last(ga, za, q2a, CUT_A[0], hops_a0, x)
-    pair_last(gb, xb, q2b, CUT_B[0], hops_b0, z)
-    hops_a1 = pair_two(ga, *pair_a, CUT_A[1], hops_a1, X, xp, xm)
-    hops_b1 = pair_two(gb, *pair_b, CUT_B[1], hops_b1, Z, zp, zm)
     for copy in bias_x:
         copy.wait_recv()
     by[y] = (bx[0] + bx[1]) + (bx[2] + bx[3])
     bias_y = remote(by.at[y], by.at[y], Y, yo)
+    pair_last(gb, xb, q2b, CUT_B[0], hops_b0, z)
+    pair_last(ga, za, q2a, CUT_A[0], hops_a0, x)
+    pair_last(gb, xb, q2b, CUT_B[1], hops_b1, z)
+    end_b = remote(gb.at[xb, 2 * z + yo], ryb, Y, yo)
     pair_last(ga, za, q2a, CUT_A[1], hops_a1, x)
     end_a = remote(ga.at[za, 2 * x + yo], rya, Y, yo)
-    pair_last(gb, xb, q2b, CUT_B[1], hops_b1, z)
-    end_b = remote(gb.at[xb, 2 * z + yo], ryb, Y, yo)
     returned(1)
 
     end_a.wait_recv()
@@ -510,7 +524,7 @@
         vm((2, 4, *unit_b), BF16), vm((2, 8, *unit_b), BF16),
         vm((2, *unit_a), BF16), vm((2, 2, *unit_a), BF16), vm(unit_a, BF16),
         vm((2, *unit_b), BF16), vm((2, 2, *unit_b), BF16), vm(unit_b, BF16),
-        vm((GROUP, WB), F32), vm((512, 640), F32), vm((ROWS, FEAT), F32),
+        vm((GROUP, WB), F32), vm((512, 256), F32), vm((512, 256), F32), vm((ROWS, FEAT), F32),
         vm((1, FEAT), F32), vm((1, FEAT), F32),
         vm((2, 1, FEAT), F32), vm((4, 1, FEAT), F32), vm((4, 1, FEAT), F32),
         vm((2, 1, FEAT), F32), vm((FEAT,), F32), vm((FEAT,), F32),

time: 140 us -> 131 us (0.936)
  Pallas kernels: 139 us -> 130 us
    pallas_call x1, Pallas kernels: 133 us -> 124 us  [shards(): pl.pallas_call(kernel, out_shape=(jax.ShapeDtypeStruct(hidden_grad.shape,...]
where the time goes in v3:
time: 131 us
  Pallas kernels  130 us (99%)
    pallas_call x1, Pallas kernels, shards(): pl.pallas_call(kernel, out_shape=(jax.ShapeDtypeStruct(hidden_grad.shape,...  124 us
    pallas_call x1, Pallas kernels, shards(): pl.pallas_call(handed_on, out_shape=tuple((jax.ShapeDtypeStruct(r.shape,...  5.83 us

profile of v3, /device:TPU:0, one launch (start us, length us, event | category | flops | bytes accessed | tf_op | source)
XLA Modules:
  0.0 131.0 jit_solution(9108957787560049541)
XLA Ops:
  0.6 124.4 %shard_map.92 = (bf16[2,512,2176]{2,1,0:T(8,128)(2,1)}, f32[34,2176]{1,0:T(8,128)}, f32[2176]{0:T(1024)}, bf16[2,1,256,1024]{3,2,1,0:T(8,128)(2,1)}, bf16[2,1,256,1152]{3,2,1,0:T(8,128)(2,1)}) custom-call(bf16[2,1,256,1024]{3,2,1,0:T(8,128)(2,1)} %dino.1, bf16[2,1,256,1152]{3,2,1,0:T(8,128)(2,1)} %siglip.1, bf16[34,2176]{1,0:T(8,128)(2,1)} %w.1, ...), custom_call_target="tpu_custom_call" | custom-call | flops 29091692544 | bytes 20971520 | tf_op jit(solution)/shard_map/pallas_call | solution.py:535
  125.0 5.8 %shard_map.93 = (bf16[2,512,2176]{2,1,0:T(8,128)(2,1)}, f32[34,2176]{1,0:T(8,128)}, f32[2176]{0:T(1024)}, bf16[2,1,256,1024]{3,2,1,0:T(8,128)(2,1)}, bf16[2,1,256,1152]{3,2,1,0:T(8,128)(2,1)}) custom-call(bf16[2,512,2176]{2,1,0:T(8,128)(2,1)} %get-tuple-element.10.refs_0_, f32[34,2176]{1,0:T(8,128)} %get-tuple-element.11.refs_1_, ...), custom_call_target="tpu_custom_call" | custom-call | bytes 14680064 | tf_op jit(solution)/shard_map/pallas_call | solution.py:554

commit v4 on v3

--- a/solution.py
+++ b/solution.py
@@ -29,7 +29,7 @@
     hidden, wgrad, bgrad, dino_grad, siglip_grad,
     ga, gb, wd, f, ft, lg, hid, fsend, frecv,
     rca, rcb, r1a, r2a, r1b, r2b, q1a, q2a, rya, q1b, q2b, ryb,
-    scr, pre, pre_next, wout, bias, bsum, bc, bz, bx, by, flat_in, flat_out,
+    scr, scr_next, pre, pre_next, wout, bias, bsum, bc, bz, bx, by, flat_in, flat_out,
     ssem, rsem, lsem,
 ):
     e, x, y, z, c = (lax.axis_index(n) for n in (E, X, Y, Z, C))
@@ -308,15 +308,23 @@
         width = cols.stop - cols.start
         at = slice(cols.start + (WA if buf is gb else 0), cols.stop + (WA if buf is gb else 0))
 
-        def step(g, carry):
+        def product(g, slot):
             rows = pl.ds(pl.multiple_of(g * GROUP, 16), GROUP)
-            scr[:, 0:width] = jnp.dot(ft[rows, :], lg[:, at], preferred_element_type=F32)
+            slot[:, 0:width] = jnp.dot(ft[rows, :], lg[:, at], preferred_element_type=F32)
+
+        def laid_out(g, slot):
             for j in range(8):
                 i, k = where_b(g, j) if buf is gb else (j, g)
-                buf[i, k, :, cols] = scr[j * ROWS:(j + 1) * ROWS, 0:width].astype(BF16)
+                buf[i, k, :, cols] = slot[j * ROWS:(j + 1) * ROWS, 0:width].astype(BF16)
+
+        def step(p, carry):
+            product(2 * p, scr)
+            product(2 * p + 1, scr_next)
+            laid_out(2 * p, scr)
+            laid_out(2 * p + 1, scr_next)
             return carry
 
-        lax.fori_loop(0, 8, step, 0)
+        lax.fori_loop(0, 4, step, 0)
 
     def core_part(buf, rc, cols, order):
         weight_part(buf, cols)
@@ -524,7 +532,7 @@
         vm((2, 4, *unit_b), BF16), vm((2, 8, *unit_b), BF16),
         vm((2, *unit_a), BF16), vm((2, 2, *unit_a), BF16), vm(unit_a, BF16),
         vm((2, *unit_b), BF16), vm((2, 2, *unit_b), BF16), vm(unit_b, BF16),
-        vm((GROUP, WB), F32), vm((512, 256), F32), vm((512, 256), F32), vm((ROWS, FEAT), F32),
+        vm((GROUP, 640), F32), vm((GROUP, 640), F32), vm((512, 256), F32), vm((512, 256), F32), vm((ROWS, FEAT), F32),
         vm((1, FEAT), F32), vm((1, FEAT), F32),
         vm((2, 1, FEAT), F32), vm((4, 1, FEAT), F32), vm((4, 1, FEAT), F32),
         vm((2, 1, FEAT), F32), vm((FEAT,), F32), vm((FEAT,), F32),

time: 131 us -> 128 us (0.977)
  Pallas kernels: 130 us -> 128 us
    pallas_call x1, Pallas kernels: 124 us -> 122 us  [shards(): pl.pallas_call(kernel, out_shape=(jax.ShapeDtypeStruct(hidden_grad.shape,...]
where the time goes in v4:
time: 128 us
  Pallas kernels  128 us (100%)
    pallas_call x1, Pallas kernels, shards(): pl.pallas_call(kernel, out_shape=(jax.ShapeDtypeStruct(hidden_grad.shape,...  122 us
    pallas_call x1, Pallas kernels, shards(): pl.pallas_call(handed_on, out_shape=tuple((jax.ShapeDtypeStruct(r.shape,...  5.83 us

profile of v4, /device:TPU:0, one launch (start us, length us, event | category | flops | bytes accessed | tf_op | source)
XLA Modules:
  0.0 128.3 jit_solution(1045476390257440818)
XLA Ops:
  0.6 121.7 %shard_map.92 = (bf16[2,512,2176]{2,1,0:T(8,128)(2,1)}, f32[34,2176]{1,0:T(8,128)}, f32[2176]{0:T(1024)}, bf16[2,1,256,1024]{3,2,1,0:T(8,128)(2,1)}, bf16[2,1,256,1152]{3,2,1,0:T(8,128)(2,1)}) custom-call(bf16[2,1,256,1024]{3,2,1,0:T(8,128)(2,1)} %dino.1, bf16[2,1,256,1152]{3,2,1,0:T(8,128)(2,1)} %siglip.1, bf16[34,2176]{1,0:T(8,128)(2,1)} %w.1, ...), custom_call_target="tpu_custom_call" | custom-call | flops 29091692544 | bytes 20971520 | tf_op jit(solution)/shard_map/pallas_call | solution.py:543
  122.4 5.8 %shard_map.93 = (bf16[2,512,2176]{2,1,0:T(8,128)(2,1)}, f32[34,2176]{1,0:T(8,128)}, f32[2176]{0:T(1024)}, bf16[2,1,256,1024]{3,2,1,0:T(8,128)(2,1)}, bf16[2,1,256,1152]{3,2,1,0:T(8,128)(2,1)}) custom-call(bf16[2,512,2176]{2,1,0:T(8,128)(2,1)} %get-tuple-element.10.refs_0_, f32[34,2176]{1,0:T(8,128)} %get-tuple-element.11.refs_1_, ...), custom_call_target="tpu_custom_call" | custom-call | bytes 14680064 | tf_op jit(solution)/shard_map/pallas_call | solution.py:562
